TPU v7x, 32 devices: a whole 2x2x4 slice. The times are simulated.
32 devices in a mesh: seq: 4 (over x, core), batch: 8 (over z, y).
Axes of the slice: x: 2, y: 2, z: 4, core: 2. Of those that a mesh axis runs over, the one named last changes fastest.
Arguments:
- residual: float32 [8, 2048, 767], P('batch', 'seq'), may hold values from -6 to 6
- documents: int32 [8, 2048], P('batch', 'seq'), may hold values from 1 to 16383, as said below
- gain_one: float32 [768], replicated, may hold values from 0.25 to 1.75
- gain_two: float32 [768], replicated, may hold values from 0.25 to 1.75
- w_qkv: bfloat16 [768, 2304], replicated, may hold values from -0.3125 to 0.3125
- w_out: bfloat16 [768, 768], replicated, may hold values from -0.4375 to 0.4375
- w_up: bfloat16 [768, 3072], replicated, may hold values from -0.21875 to 0.21875
- w_down: bfloat16 [3072, 768], replicated, may hold values from -0.109375 to 0.109375
- cotangent: float32 [8, 2048, 767], P('batch', 'seq'), may hold values from -6 to 6
Outputs:
- new_residual: float32 [8, 2048, 767], P('batch', 'seq')
- residual_grad: float32 [8, 2048, 767], P('batch', 'seq')
- gain_one_grad: float32 [768], P('seq')
- gain_two_grad: float32 [768], P('seq')
- w_qkv_grad: float32 [768, 2304], P('seq')
- w_out_grad: float32 [768, 768], P('seq')
- w_up_grad: float32 [768, 3072], P('seq')
- w_down_grad: float32 [3072, 768], P('seq')
Inputs may be any that keep to these rules, and one draw needn't show every extreme that they name: `documents`: every document is one unbroken run within a row, or the end of one row's last document followed by the start of the next row's first; the last row's last document, with id 8 * 2048 - 1, continues at the start of the first row. Within a row, ids after its first document rise. A continued document lies within the last 512 positions of the earlier row and the first 512 positions of the later one. No other document has tokens in two rows. In every row some document begins within its first 512 positions and ends within its last 512.
All inputs are finite; a program needn't handle non-finite values.
Results may differ from a plain program's by a relative error of at most 0.04.
Values may be sent and summed in bfloat16 or wider, within the bound.
A program may use at most 192 MiB of HBM per device.

v0:
```python
import math

import jax
import jax.numpy as jnp
from jax import lax
from jax.sharding import PartitionSpec as P

H = 12
HD = 64


EPSILON = 1e-06
MASKED = -1e30


def passed_along(block, axis, distance):
    devices = range(lax.axis_size(axis))
    route = [((i - distance) % len(devices), i) for i in devices]
    return lax.ppermute(block, axis, route)


def expand(narrow):
    return jnp.concatenate([narrow, -jnp.sum(narrow, axis=-1, keepdims=True)], axis=-1)


def shrink(full_vec):
    return full_vec[..., :-1] - jnp.mean(full_vec, axis=-1, keepdims=True)


def shrink_back(grad_narrow):
    padded = jnp.concatenate([grad_narrow, jnp.zeros_like(grad_narrow[..., :1])], axis=-1)
    return padded - jnp.sum(grad_narrow, axis=-1, keepdims=True) / padded.shape[-1]


def crms_norm(narrow, gain_vec):
    full_vec = expand(narrow)
    return (
        gain_vec
        * full_vec
        * lax.rsqrt(jnp.mean(full_vec * full_vec, axis=-1, keepdims=True) + EPSILON)
    )


def visible(query_docs, query_pos, key_docs, key_pos):
    return (query_docs[:, None] == key_docs[None, :]) & (key_pos[None, :] <= query_pos[:, None])


def per_device(residual, documents, gain_one, gain_two, w_qkv, w_out, w_up, w_down, cotangent):
    seq_count = lax.axis_size("seq")
    seq_place = lax.axis_index("seq")
    narrow = residual[0]
    query_docs = documents[0]
    tok_rows = narrow.shape[0]
    width = w_out.shape[0]
    scale = 1.0 / math.sqrt(HD)
    query_pos = seq_place * tok_rows + jnp.arange(tok_rows, dtype=jnp.int32)
    h_one = crms_norm(narrow, gain_one).astype(jnp.bfloat16)
    packed = jnp.dot(h_one, w_qkv, preferred_element_type=jnp.float32).astype(jnp.bfloat16)
    queries = packed[:, :width].reshape(tok_rows, H, HD)
    key_rows = packed[:, width : 2 * width]
    value_rows = packed[:, 2 * width :]
    near_keys, near_values, near_docs = (
        lax.all_gather(key_rows, "seq", axis=0, tiled=True),
        lax.all_gather(value_rows, "seq", axis=0, tiled=True),
        lax.all_gather(query_docs, "seq", axis=0, tiled=True),
    )
    row_tail = seq_count * tok_rows - tok_rows
    prior_keys, prior_values, prior_docs = passed_along(
        (near_keys[row_tail:], near_values[row_tail:], near_docs[row_tail:]), "batch", 1
    )
    blocks = seq_count + 1
    key_stack = jnp.concatenate(
        [prior_keys[None], near_keys.reshape(seq_count, tok_rows, width)]
    ).reshape(blocks, tok_rows, H, HD)
    value_stack = jnp.concatenate(
        [prior_values[None], near_values.reshape(seq_count, tok_rows, width)]
    ).reshape(blocks, tok_rows, H, HD)
    doc_stack = jnp.concatenate([prior_docs[None], near_docs.reshape(seq_count, tok_rows)])
    pos_stack = jnp.concatenate(
        [
            jnp.full((1, tok_rows), -1, jnp.int32),
            jnp.arange(seq_count * tok_rows, dtype=jnp.int32).reshape(seq_count, tok_rows),
        ]
    )
    stacks = (key_stack, value_stack, doc_stack, pos_stack)

    def score_block(key_block):
        return (
            jnp.einsum("qhd,khd->hqk", queries, key_block, preferred_element_type=jnp.float32)
            * scale
        )

    def lse_step(carry, key_set):
        key_block, value_block, key_docs, key_pos = key_set
        pairs = visible(query_docs, query_pos, key_docs, key_pos)
        running_max, running_sum = carry
        scores = jnp.where(pairs[None], score_block(key_block), MASKED)
        new_max = jnp.maximum(running_max, jnp.max(scores, axis=-1))
        new_sum = running_sum * jnp.exp(running_max - new_max) + jnp.sum(
            jnp.where(pairs[None], jnp.exp(scores - new_max[:, :, None]), 0.0), axis=-1
        )
        return ((new_max, new_sum), None)

    start_state = (
        jnp.full((H, tok_rows), MASKED, jnp.float32),
        jnp.zeros((H, tok_rows), jnp.float32),
    )
    (running_max, running_sum), _ = lax.scan(lse_step, start_state, stacks)
    log_total = running_max + jnp.log(running_sum)

    def probs_of(key_block, pairs):
        return jnp.where(pairs[None], jnp.exp(score_block(key_block) - log_total[:, :, None]), 0.0)

    def out_step(carry, key_set):
        key_block, value_block, key_docs, key_pos = key_set
        pairs = visible(query_docs, query_pos, key_docs, key_pos)
        summed, leftover = carry
        attn_probs = probs_of(key_block, pairs)
        probs_low = attn_probs.astype(jnp.bfloat16)
        remainder = (attn_probs - probs_low.astype(jnp.float32)).astype(jnp.bfloat16)
        new_summed = summed + jnp.einsum(
            "hqk,khd->qhd", probs_low, value_block, preferred_element_type=jnp.float32
        )
        new_leftover = leftover + jnp.einsum(
            "hqk,khd->qhd", remainder, value_block, preferred_element_type=jnp.float32
        )
        return ((new_summed, new_leftover), None)

    empty_heads = jnp.zeros(queries.shape, jnp.float32)
    (attended_full, leftover_full), _ = lax.scan(out_step, (empty_heads, empty_heads), stacks)
    attended = attended_full.reshape(tok_rows, width).astype(jnp.bfloat16)
    branch_one = jnp.dot(attended, w_out, preferred_element_type=jnp.float32)
    middle = narrow + shrink(branch_one)
    h_two = crms_norm(middle, gain_two).astype(jnp.bfloat16)
    up_proj = jnp.dot(h_two, w_up, preferred_element_type=jnp.float32)
    gelu_out = jax.nn.gelu(up_proj).astype(jnp.bfloat16)
    branch_two = jnp.dot(gelu_out, w_down, preferred_element_type=jnp.float32)
    new_residual = middle + shrink(branch_two)
    grad_new = cotangent[0]
    grad_two = shrink_back(grad_new).astype(jnp.bfloat16)
    grad_w_down = jnp.einsum("tf,td->fd", gelu_out, grad_two, preferred_element_type=jnp.float32)
    grad_gelu = jnp.einsum("td,fd->tf", grad_two, w_down, preferred_element_type=jnp.float32)
    _, gelu_pull = jax.vjp(jax.nn.gelu, up_proj)
    grad_up = gelu_pull(grad_gelu)[0].astype(jnp.bfloat16)
    grad_w_up = jnp.einsum("td,tf->df", h_two, grad_up, preferred_element_type=jnp.float32)
    grad_h_two = jnp.einsum("tf,df->td", grad_up, w_up, preferred_element_type=jnp.float32)
    _, norm_pull_two = jax.vjp(crms_norm, middle, gain_two)
    grad_middle_norm, grad_gain_two = norm_pull_two(grad_h_two)
    grad_middle = grad_new + grad_middle_norm
    grad_one = shrink_back(grad_middle).astype(jnp.bfloat16)
    grad_w_out = jnp.einsum("td,te->de", attended, grad_one, preferred_element_type=jnp.float32)
    grad_attended_flat = jnp.einsum(
        "te,de->td", grad_one, w_out, preferred_element_type=jnp.float32
    ).astype(jnp.bfloat16)
    grad_attended = grad_attended_flat.reshape(tok_rows, H, HD)
    exact_mix = attended_full + leftover_full
    delta = jnp.sum(grad_attended.astype(jnp.float32) * exact_mix, axis=-1).T

    def query_terms(key_block, value_block, pairs):
        attn_probs = probs_of(key_block, pairs)
        grad_probs = jnp.einsum(
            "qhd,khd->hqk", grad_attended, value_block, preferred_element_type=jnp.float32
        )
        grad_scores = (attn_probs * (grad_probs - delta[:, :, None]) * scale).astype(jnp.bfloat16)
        return (attn_probs, grad_scores)

    def query_step(summed, key_set):
        key_block, value_block, key_docs, key_pos = key_set
        pairs = visible(query_docs, query_pos, key_docs, key_pos)
        attn_probs, grad_scores = query_terms(key_block, value_block, pairs)
        return (
            summed
            + jnp.einsum(
                "hqk,khd->qhd", grad_scores, key_block, preferred_element_type=jnp.float32
            ),
            None,
        )

    grad_query, _ = lax.scan(query_step, empty_heads, stacks)
    flat_queries = packed[:, :width]
    lse_rows = log_total.T
    delta_rows = delta.T
    far_queries, far_grads = (
        lax.all_gather(flat_queries, "seq", axis=0, tiled=True),
        lax.all_gather(grad_attended_flat, "seq", axis=0, tiled=True),
    )
    far_lse, far_delta = (
        lax.all_gather(lse_rows, "seq", axis=0, tiled=True),
        lax.all_gather(delta_rows, "seq", axis=0, tiled=True),
    )
    next_queries, next_grads = passed_along(
        (far_queries[:tok_rows], far_grads[:tok_rows]), "batch", -1
    )
    next_lse, next_delta, next_docs = passed_along(
        (far_lse[:tok_rows], far_delta[:tok_rows], near_docs[:tok_rows]), "batch", -1
    )
    query_stack = jnp.concatenate(
        [far_queries.reshape(seq_count, tok_rows, width), next_queries[None]]
    ).reshape(blocks, tok_rows, H, HD)
    outgrad_stack = jnp.concatenate(
        [far_grads.reshape(seq_count, tok_rows, width), next_grads[None]]
    ).reshape(blocks, tok_rows, H, HD)
    lse_stack = jnp.concatenate([far_lse.reshape(seq_count, tok_rows, H), next_lse[None]])
    delta_stack = jnp.concatenate([far_delta.reshape(seq_count, tok_rows, H), next_delta[None]])
    qdoc_stack = jnp.concatenate([near_docs.reshape(seq_count, tok_rows), next_docs[None]])
    qpos_stack = jnp.concatenate(
        [
            jnp.arange(seq_count * tok_rows, dtype=jnp.int32).reshape(seq_count, tok_rows),
            (seq_count * tok_rows + jnp.arange(tok_rows, dtype=jnp.int32))[None],
        ]
    )
    own_keys = key_rows.reshape(tok_rows, H, HD)
    own_values = value_rows.reshape(tok_rows, H, HD)

    def key_step(carry, query_set):
        query_block, outgrad_block, lse_block, delta_block, block_docs, block_pos = query_set
        pairs = visible(block_docs, block_pos, query_docs, query_pos)
        key_sum, value_sum = carry
        scores = (
            jnp.einsum("qhd,khd->hqk", query_block, own_keys, preferred_element_type=jnp.float32)
            * scale
        )
        attn_probs = jnp.where(pairs[None], jnp.exp(scores - lse_block.T[:, :, None]), 0.0)
        grad_probs = jnp.einsum(
            "qhd,khd->hqk", outgrad_block, own_values, preferred_element_type=jnp.float32
        )
        grad_scores = (attn_probs * (grad_probs - delta_block.T[:, :, None]) * scale).astype(
            jnp.bfloat16
        )
        new_key = key_sum + jnp.einsum(
            "hqk,qhd->khd", grad_scores, query_block, preferred_element_type=jnp.float32
        )
        new_value = value_sum + jnp.einsum(
            "hqk,qhd->khd",
            attn_probs.astype(jnp.bfloat16),
            outgrad_block,
            preferred_element_type=jnp.float32,
        )
        return ((new_key, new_value), None)

    (key_grad_heads, value_grad_heads), _ = lax.scan(
        key_step,
        (empty_heads, empty_heads),
        (query_stack, outgrad_stack, lse_stack, delta_stack, qdoc_stack, qpos_stack),
    )
    key_grad_total = key_grad_heads.reshape(tok_rows, width)
    value_grad_total = value_grad_heads.reshape(tok_rows, width)
    grad_packed = jnp.concatenate(
        [grad_query.reshape(tok_rows, width), key_grad_total, value_grad_total], axis=1
    ).astype(jnp.bfloat16)
    grad_w_qkv = jnp.einsum("td,tf->df", h_one, grad_packed, preferred_element_type=jnp.float32)
    grad_h_one = jnp.einsum("tf,df->td", grad_packed, w_qkv, preferred_element_type=jnp.float32)
    _, norm_pull_one = jax.vjp(crms_norm, narrow, gain_one)
    grad_narrow_norm, grad_gain_one = norm_pull_one(grad_h_one)
    residual_grad = grad_middle + grad_narrow_norm
    shares = (
        lax.psum_scatter(grad_w_qkv, "seq", scatter_dimension=0, tiled=True),
        lax.psum_scatter(grad_w_out, "seq", scatter_dimension=0, tiled=True),
        lax.psum_scatter(grad_w_up, "seq", scatter_dimension=0, tiled=True),
        lax.psum_scatter(grad_w_down, "seq", scatter_dimension=0, tiled=True),
        lax.psum_scatter(grad_gain_one, "seq", scatter_dimension=0, tiled=True),
        lax.psum_scatter(grad_gain_two, "seq", scatter_dimension=0, tiled=True),
    )
    totals = lax.psum((shares[0], shares[1], shares[2], shares[3], shares[4], shares[5]), "batch")
    return (
        new_residual[None],
        residual_grad[None],
        totals[4],
        totals[5],
        totals[0],
        totals[1],
        totals[2],
        totals[3],
    )


def solution(mesh):
    placed = (
        P("batch", "seq", None),
        P("batch", "seq"),
        P(),
        P(),
        P(),
        P(),
        P(),
        P(),
        P("batch", "seq", None),
    )
    return jax.shard_map(
        per_device,
        mesh=mesh,
        in_specs=placed,
        out_specs=(
            P("batch", "seq", None),
            P("batch", "seq", None),
            P("seq"),
            P("seq"),
            P("seq", None),
            P("seq", None),
            P("seq", None),
            P("seq", None),
        ),
        check_vma=False,
    )
```

profile of v0, /device:TPU:0, one launch (start us, length us, event | category | flops | bytes accessed | tf_op | source)
XLA Modules:
  0.0 1079.6 jit_solution(11624071718494662098)
XLA Ops:
  29.9 24.5 %all-gather.8.cloned.1.call-done = bf16[2048,768]{1,0:T(8,128)(2,1)} async-done(((bf16[512,768]{1,0:T(8,128)(2,1)}), bf16[2048,768]{1,0:T(8,128)(2,1)}) %all-gather.8.cloned.1.call-update) | async-done | bytes 3145744 | tf_op jit(solution)/shard_map/all_gather | solution.py:63
  117.4 91.5 %while.50 = (s32[]{:T(128)}, f32[12,512]{1,0:T(8,128)}, f32[12,512]{1,0:T(8,128)}, s32[1,512]{1,0:T(1,128)S(1)}, s32[5,512]{1,0:T(8,128)}, /*index=5*/s32[5,512]...) while((s32[]{:T(128)}, f32[12,512]{1,0:T(8,128)}, ...), condition=%wide.region_5.6_spmd.clone, body=%wide.region_2.5_spmd.clone.sunk | while | flops 428636672 | bytes 29207280 | solution.py:108
  118.5 8.6 fusion.169
  136.8 8.6 fusion.169
  155.1 8.6 fusion.169
  173.4 8.6 fusion.169
  191.7 8.6 fusion.169
  222.3 122.9 %while.51 = (s32[]{:T(128)}, f32[512,12,64]{0,2,1:T(8,128)}, f32[512,12,64]{0,2,1:T(8,128)}, bf16[5,512,12,64]{1,3,2,0:T(8,128)(2,1)}, s32[1,512]{1,0:T(1,128)S(...) while((s32[]{:T(128)}, f32[512,12,64]{0,2,1:T(8,128)}, ...), condition=%wide.region_7.8_spmd.clone, body=%wide.region_6.7_spmd.clone.sunk | while | flops 1244922368 | bytes 99528416 | solution.py:130
  232.0 9.7 bitcast_add_fusion.11
  255.9 10.2 bitcast_add_fusion.11
  280.6 10.2 bitcast_add_fusion.11
  305.3 10.2 bitcast_add_fusion.11
  330.0 10.2 bitcast_add_fusion.11
  359.3 9.9 fusion.97
  380.7 8.8 fusion.115
  418.0 9.8 fusion.112
  430.0 111.8 %while.52 = (s32[]{:T(128)}, f32[512,12,64]{0,2,1:T(8,128)}, bf16[5,512,12,64]{1,3,2,0:T(8,128)(2,1)}, s32[1,512]{1,0:T(1,128)S(1)}, s32[5,512]{1,0:T(8,128)}, /...) while((s32[]{:T(128)}, f32[512,12,64]{0,2,1:T(8,128)}, ...), condition=%wide.region_17.18_spmd.clone, body=%wide.region_16.17_spmd.clone.sunk | while | flops 1231553024 | bytes 32853652 | solution.py:179
  439.5 11.8 %bitcast_add_fusion.12 = f32[512,12,64]{0,2,1:T(8,128)} fusion(f32[512,12,64]{0,2,1:T(8,128)} %get-tuple-element.1120, f32[12,512,512]{2,1,0:T(8,128)} %fusion.183, f32[12,512]{1,0:T(8,128)} %get-tuple-element.1143, f32[12,512]{1,0:T(8,128)} %get-tuple-element.1140, pred[512,512]{0,1:T(8,128)(4,1)} %compare_and_fusion.10, ...), kind=kOutput, calls=%fused_computation.55.clone.1 | convolution fusion | flops 828112896 | bytes 18416640 | tf_op jit(solution)/shard_map/while/body/eval_jaxpr/hqk,khd->qhd/dot_general | solution.py:173
  453.0 9.4 fusion.183
  462.4 12.3 %bitcast_add_fusion.12 = f32[512,12,64]{0,2,1:T(8,128)} fusion(f32[512,12,64]{0,2,1:T(8,128)} %get-tuple-element.1120, f32[12,512,512]{2,1,0:T(8,128)} %fusion.183, f32[12,512]{1,0:T(8,128)} %get-tuple-element.1143, f32[12,512]{1,0:T(8,128)} %get-tuple-element.1140, pred[512,512]{0,1:T(8,128)(4,1)} %compare_and_fusion.10, ...), kind=kOutput, calls=%fused_computation.55.clone.1 | convolution fusion | flops 828112896 | bytes 18416640 | tf_op jit(solution)/shard_map/while/body/eval_jaxpr/hqk,khd->qhd/dot_general | solution.py:173
  484.1 12.6 %bitcast_add_fusion.12 = f32[512,12,64]{0,2,1:T(8,128)} fusion(f32[512,12,64]{0,2,1:T(8,128)} %get-tuple-element.1120, f32[12,512,512]{2,1,0:T(8,128)} %fusion.183, f32[12,512]{1,0:T(8,128)} %get-tuple-element.1143, f32[12,512]{1,0:T(8,128)} %get-tuple-element.1140, pred[512,512]{0,1:T(8,128)(4,1)} %compare_and_fusion.10, ...), kind=kOutput, calls=%fused_computation.55.clone.1 | convolution fusion | flops 828112896 | bytes 18416640 | tf_op jit(solution)/shard_map/while/body/eval_jaxpr/hqk,khd->qhd/dot_general | solution.py:173
  506.1 12.4 %bitcast_add_fusion.12 = f32[512,12,64]{0,2,1:T(8,128)} fusion(f32[512,12,64]{0,2,1:T(8,128)} %get-tuple-element.1120, f32[12,512,512]{2,1,0:T(8,128)} %fusion.183, f32[12,512]{1,0:T(8,128)} %get-tuple-element.1143, f32[12,512]{1,0:T(8,128)} %get-tuple-element.1140, pred[512,512]{0,1:T(8,128)(4,1)} %compare_and_fusion.10, ...), kind=kOutput, calls=%fused_computation.55.clone.1 | convolution fusion | flops 828112896 | bytes 18416640 | tf_op jit(solution)/shard_map/while/body/eval_jaxpr/hqk,khd->qhd/dot_general | solution.py:173
  527.9 13.9 %bitcast_add_fusion.12 = f32[512,12,64]{0,2,1:T(8,128)} fusion(f32[512,12,64]{0,2,1:T(8,128)} %get-tuple-element.1120, f32[12,512,512]{2,1,0:T(8,128)} %fusion.183, f32[12,512]{1,0:T(8,128)} %get-tuple-element.1143, f32[12,512]{1,0:T(8,128)} %get-tuple-element.1140, pred[512,512]{0,1:T(8,128)(4,1)} %compare_and_fusion.10, ...), kind=kOutput, calls=%fused_computation.55.clone.1 | convolution fusion | flops 828112896 | bytes 18416640 | tf_op jit(solution)/shard_map/while/body/eval_jaxpr/hqk,khd->qhd/dot_general | solution.py:173
  607.7 144.9 %while.53 = (s32[]{:T(128)}, f32[512,12,64]{0,2,1:T(8,128)}, f32[512,12,64]{0,2,1:T(8,128)}, bf16[5,512,12,64]{1,3,2,0:T(8,128)(2,1)}, s32[5,512]{1,0:T(8,128)},...) while((s32[]{:T(128)}, f32[512,12,64]{0,2,1:T(8,128)}, ...), condition=%wide.region_19.20_spmd.clone, body=%wide.region_18.19_spmd.clone.sunk | while | flops 1647575552 | bytes 49762464 | solution.py:241
  626.6 9.9 bitcast_add_fusion.13
  655.5 10.1 bitcast_add_fusion.13
  684.5 10.1 bitcast_add_fusion.13
  713.5 10.1 bitcast_add_fusion.13
  742.6 10.1 bitcast_add_fusion.13
  762.4 63.2 %reduce-scatter.5.cloned.1.call-done = f32[192,2304]{1,0:T(8,128)} async-done(((f32[768,2304]{1,0:T(8,128)}), f32[192,2304]{1,0:T(8,128)}) %reduce-scatter.5.cloned.1.call-update) | async-done | bytes 1769488 | tf_op jit(solution)/shard_map/reduce_scatter | solution.py:257
  866.1 23.0 %all-reduce.5 = (f32[192]{0:T(256)}, f32[192]{0:T(256)}) all-reduce(f32[192]{0:T(256)S(1)} %dynamic-slice.1, f32[192]{0:T(256)S(1)} %copy-done.39), channel_id=1, replica_groups=mesh['seq'=4,'batch'=8] {'batch'}, use_global_device_ids=true, to_apply=%region_23.24 | all-reduce | flops 384 | bytes 3072 | tf_op jit(solution)/shard_map/psum | solution.py:264
  889.2 177.1 %all-reduce.10.cloned.1.call-done = (f32[192,2304]{1,0:T(8,128)}, f32[192,768]{1,0:T(8,128)}, f32[192,3072]{1,0:T(8,128)}, f32[768,768]{1,0:T(8,128)}) async-done(((f32[192,2304]{1,0:T(8,128)}, f32[192,768]{1,0:T(8,128)}, f32[192,3072]{1,0:T(8,128)}, f32[768,768]{1,0:T(8,128)}), (f32[192,2304]{1,0:T(8,128)}, f32[192,768]{1,0:T(8,128)}, f32[192,3072]{1,0:T(8,128)}, ...) | async-done | bytes 7077904 | tf_op jit(solution)/shard_map/psum | solution.py:264
  (410 shorter events, 531.0 us)
Async XLA Ops:
  7.2 10.7 copy-start
  7.2 10.7 copy-start.36
  7.2 47.1 %all-gather.8.cloned.1.call-start = ((), (), s32[]{:S(2)}) async-start(), calls=%async_computation.5 | async-start | bytes 3932160 | tf_op jit(solution)/shard_map/all_gather | solution.py:63
  22.9 68.4 %all-gather.6.cloned.1.call-start = ((), (), s32[]{:S(2)}) async-start(), calls=%async_computation.4 | async-start | bytes 3932160 | tf_op jit(solution)/shard_map/all_gather | solution.py:64
  23.7 370.5 %all-gather.10.cloned.1.call-start = ((), (), s32[]{:S(2)}) async-start(), calls=%async_computation.6 | async-start | bytes 3932160 | tf_op jit(solution)/shard_map/all_gather | solution.py:184
  56.4 48.0 %collective-permute-start.2 = (bf16[512,768]{1,0:T(8,128)(2,1)}, bf16[512,768]{1,0:T(8,128)(2,1)}, u32[]{:S(2)}, u32[]{:S(2)}) collective-permute-start(bf16[512,768]{1,0:T(8,128)(2,1)} %slice.59), channel_id=1, source_target_pairs={{7,0},{0,1},{1,2},{2,3},{3,4},{4,5},{5,6},{6,7},{15,8},{8,9},{9,10... | collective-permute-start | bytes 2359304 | tf_op jit(solution)/shard_map/ppermute | solution.py:19
  58.5 16.7 %collective-permute-start.4 = (s32[512]{0:T(512)}, s32[512]{0:T(512)}, u32[]{:S(2)}, u32[]{:S(2)}) collective-permute-start(s32[512]{0:T(512)} %bitcast.15), channel_id=1, source_target_pairs={{1,0},{2,1},{3,2},{4,3},{5,4},{6,5},{7,6},{0,7},{9,8},{10,9},{11,1... | collective-permute-start | bytes 6152 | tf_op jit(solution)/shard_map/ppermute | solution.py:19
  61.7 17.5 %collective-permute-start.1 = (s32[512]{0:T(512)}, s32[512]{0:T(512)}, u32[]{:S(2)}, u32[]{:S(2)}) collective-permute-start(s32[512]{0:T(512)} %bitcast.3), channel_id=1, source_target_pairs={{7,0},{0,1},{1,2},{2,3},{3,4},{4,5},{5,6},{6,7},{15,8},{8,9},{9,10... | collective-permute-start | bytes 6152 | tf_op jit(solution)/shard_map/ppermute | solution.py:19
  61.7 366.1 %all-gather.12.cloned.1.call-start = ((), (), s32[]{:S(2)}) async-start(), calls=%async_computation.7 | async-start | bytes 3932160 | tf_op jit(solution)/shard_map/all_gather | solution.py:185
  104.4 104.5 %collective-permute-start = (bf16[512,768]{1,0:T(8,128)(2,1)}, bf16[512,768]{1,0:T(8,128)(2,1)}, u32[]{:S(2)}, u32[]{:S(2)}) collective-permute-start(bf16[512,768]{1,0:T(8,128)(2,1)} %slice.56), channel_id=1, source_target_pairs={{7,0},{0,1},{1,2},{2,3},{3,4},{4,5},{5,6},{6,7},{15,8},{8,9},{9,10... | collective-permute-start | bytes 2359304 | tf_op jit(solution)/shard_map/ppermute | solution.py:19
  255.9 10.2 copy-start.9
  255.9 10.2 copy-start.31
  280.6 10.2 copy-start.1
  280.6 10.2 copy-start.9
  280.6 10.2 copy-start.31
  305.3 10.2 copy-start.9
  305.3 10.2 copy-start.31
  330.0 10.2 copy-start.1
  330.0 10.2 copy-start.9
  330.0 10.2 copy-start.31
  353.9 15.3 %slice-start = ((s8[4718592]{0:T(1024)(128)(4,1)}), s8[4194304]{0:T(1024)(128)(4,1)S(1)}, s32[]{:S(2)}) async-start(s8[4718592]{0:T(1024)(128)(4,1)} %bitcast.285), calls=%async_computation.13 | async-start | bytes 8388608
  376.6 385.7 %reduce-scatter.7.cloned.1.call-start = ((), (), s32[]{:S(2)}) async-start(), calls=%async_computation.9 | async-start | bytes 2949120 | tf_op jit(solution)/shard_map/reduce_scatter | solution.py:258
  380.7 381.7 %reduce-scatter.9.cloned.1.call-start = ((), (), s32[]{:S(2)}) async-start(), calls=%async_computation.10 | async-start | bytes 11796480 | tf_op jit(solution)/shard_map/reduce_scatter | solution.py:259
  389.5 372.8 %reduce-scatter.11.cloned.1.call-start = ((), (), s32[]{:S(2)}) async-start(), calls=%async_computation.11 | async-start | bytes 11796480 | tf_op jit(solution)/shard_map/reduce_scatter | solution.py:260
  407.2 10.8 copy-start.41
  407.2 161.0 %collective-permute-start.3 = (bf16[512,768]{1,0:T(8,128)(2,1)}, bf16[512,768]{1,0:T(8,128)(2,1)}, u32[]{:S(2)}, u32[]{:S(2)}) collective-permute-start(bf16[512,768]{1,0:T(8,128)(2,1)} %slice.63), channel_id=1, source_target_pairs={{1,0},{2,1},{3,2},{4,3},{5,4},{6,5},{7,6},{0,7},{9,8},{10,9},{11,1... | collective-permute-start | bytes 2359304 | tf_op jit(solution)/shard_map/ppermute | solution.py:19
  427.8 397.9 %reduce-scatter.5.cloned.1.call-start = ((), (), s32[]{:S(2)}) async-start(), calls=%async_computation.8 | async-start | bytes 8847360 | tf_op jit(solution)/shard_map/reduce_scatter | solution.py:257
  429.9 165.0 %collective-permute-start.6 = (bf16[512,768]{1,0:T(8,128)(2,1)}, bf16[512,768]{1,0:T(8,128)(2,1)}, u32[]{:S(2)}, u32[]{:S(2)}) collective-permute-start(bf16[512,768]{1,0:T(8,128)(2,1)} %slice.66), channel_id=1, source_target_pairs={{1,0},{2,1},{3,2},{4,3},{5,4},{6,5},{7,6},{0,7},{9,8},{10,9},{11,1... | collective-permute-start | bytes 2359304 | tf_op jit(solution)/shard_map/ppermute | solution.py:19
  565.5 15.7 %collective-permute-start.7 = (f32[512,12]{0,1:T(8,128)}, f32[512,12]{0,1:T(8,128)}, u32[]{:S(2)}, u32[]{:S(2)}) collective-permute-start(f32[512,12]{0,1:T(8,128)} %slice.67), channel_id=1, source_target_pairs={{1,0},{2,1},{3,2},{4,3},{5,4},{6,5},{7,6},{0,7},{9,8},{10,9},{11,1... | collective-permute-start | bytes 73736 | tf_op jit(solution)/shard_map/ppermute | solution.py:19
  568.2 14.4 %collective-permute-start.5 = (f32[512,12]{0,1:T(8,128)}, f32[512,12]{0,1:T(8,128)}, u32[]{:S(2)}, u32[]{:S(2)}) collective-permute-start(f32[512,12]{0,1:T(8,128)} %slice.65), channel_id=1, source_target_pairs={{1,0},{2,1},{3,2},{4,3},{5,4},{6,5},{7,6},{0,7},{9,8},{10,9},{11,1... | collective-permute-start | bytes 73736 | tf_op jit(solution)/shard_map/ppermute | solution.py:19
  762.3 304.0 %all-reduce.10.cloned.1.call-start = ((), (), s32[]{:S(2)}) async-start(), calls=%async_computation.12 | async-start | bytes 14155776 | tf_op jit(solution)/shard_map/psum | solution.py:264
  841.4 15.2 %copy-start.33 = (f32[512]{0:T(512)S(1)}, f32[512]{0:T(512)}, u32[]{:S(2)}) copy-start(f32[512]{0:T(512)} %copy-done.32) | copy-start | bytes 6148
  (60 other events, 311.8 us)
Sparse Core Ops, SparseCore 0:
  23.1 31.2 all-gather.7
  55.9 28.5 all-gather.5
  86.6 28.5 all-gather.9
  376.8 29.0 all-gather.11
  408.8 33.0 reduce-scatter.6
  444.5 78.3 reduce-scatter.8
  525.7 79.0 reduce-scatter.10
  762.4 63.2 reduce-scatter.4
  830.1 236.1 all-reduce.9
where the time goes:
time: 1090 us; the launch traced here: 1080 us
  matrix products  457 us (42%)
  waiting for transfers between devices  270 us (25%)
  local copies, waits for them, and re-layouts  170 us (16%)
  other arithmetic  106 us (10%)
  blocking collectives  49.8 us (5%)
  between operations  15.3 us (1%)
  starting transfers between devices  11.3 us (1%)
    psum x1, waiting for transfers between devices, per_device(): lax.psum((shares[0], shares[1], shares[2], shares[3], shares[4], shares[5...  177 us
    dot_general x15, matrix products, score_block(): jnp.einsum('qhd,khd->hqk', queries, key_block, preferred_element_type=jnp...  122 us
    reduce_scatter x1, waiting for transfers between devices, per_device(): lax.psum_scatter(grad_w_qkv, 'seq', scatter_dimension=0, tiled=True)  63.2 us
    dot_general x5, matrix products, query_step(): jnp.einsum('hqk,khd->qhd', grad_scores, key_block, preferred_element_type...  62.8 us
    dot_general x5, matrix products, out_step(): jnp.einsum('hqk,khd->qhd', remainder, value_block, preferred_element_type...  50.4 us
    dot_general x5, matrix products, key_step(): jnp.einsum('hqk,qhd->khd', grad_scores, query_block, preferred_element_ty...  50.2 us
    unnamed x95, local copies, waits for them, and re-layouts  47.1 us
    dot_general x5, matrix products, key_step(): jnp.einsum('hqk,qhd->khd', attn_probs.astype(jnp.bfloat16), outgrad_block...  40.2 us
  transfers between devices with their start and end apart: 17, of which 4 were waited for; matrix products, arithmetic and copies ran while one was open for 65% of the time, Pallas kernels for 0%

commit v1 on v0

v1 whole, which is shorter than its diff:
```python
import functools
import math

import jax
import jax.numpy as jnp
from jax import lax
from jax.experimental import pallas as pl
from jax.experimental.pallas import tpu as pltpu
from jax.sharding import PartitionSpec as P

H = 12
HD = 64
EPSILON = 1e-06
NEG = -1e30
F32, BF16 = jnp.float32, jnp.bfloat16
VMEM_LIMIT = 56 * 2**20


def passed_along(block, axis, distance):
    devices = range(lax.axis_size(axis))
    route = [((i - distance) % len(devices), i) for i in devices]
    return lax.ppermute(block, axis, route)


def expand(narrow):
    return jnp.concatenate([narrow, -jnp.sum(narrow, axis=-1, keepdims=True)], axis=-1)


def shrink(full_vec):
    return full_vec[..., :-1] - jnp.mean(full_vec, axis=-1, keepdims=True)


def shrink_back(grad_narrow):
    padded = jnp.concatenate([grad_narrow, jnp.zeros_like(grad_narrow[..., :1])], axis=-1)
    return padded - jnp.sum(grad_narrow, axis=-1, keepdims=True) / padded.shape[-1]


def crms_norm(narrow, gain_vec):
    full_vec = expand(narrow)
    return (
        gain_vec
        * full_vec
        * lax.rsqrt(jnp.mean(full_vec * full_vec, axis=-1, keepdims=True) + EPSILON)
    )


def dot(a, b):
    return lax.dot_general(a, b, (((1,), (0,)), ((), ())), preferred_element_type=F32)


def masked(s, key_docs, query_docs, key_at, query_at, causal, docs, fill):
    keep = None
    if docs:
        keep = key_docs == query_docs
    if causal:
        key_pos = lax.broadcasted_iota(jnp.int32, s.shape, 0) + key_at
        query_pos = lax.broadcasted_iota(jnp.int32, s.shape, 1) + query_at
        earlier = key_pos <= query_pos
        keep = earlier if keep is None else keep & earlier
    return s if keep is None else jnp.where(keep, s, fill)


def fwd_kernel(tok, blocks, heads, k_ref, qT_ref, vT_ref, dk_ref, dq_ref, oT_ref, lse_ref):
    def head(h, carry):
        for i in range(blocks):
            q0 = i * tok
            qT = qT_ref[h, :, q0 : q0 + tok]
            docs_q = dq_ref[:, q0 : q0 + tok]
            m = jnp.full((1, tok), NEG, F32)
            total = jnp.zeros((1, tok), F32)
            acc = jnp.zeros(qT.shape, F32)
            edge = i == 0 or i == blocks - 1
            chunks = [(0, False, True)] if i == 0 else []
            for j in range(i):
                chunks.append(((j + 1) * tok, False, j == 0 or edge))
            chunks.append(((i + 1) * tok, True, edge))
            for k0, causal, docs in chunks:
                keys = slice(k0, k0 + tok)
                s = dot(k_ref[h, keys, :], qT)
                docs_k = dk_ref[keys, :] if docs else None
                s = masked(s, docs_k, docs_q, k0 - tok, q0, causal, docs, NEG)
                new_m = jnp.maximum(m, jnp.max(s, axis=0, keepdims=True))
                p = jnp.exp(s - new_m)
                shift = jnp.exp(m - new_m)
                total = total * shift + jnp.sum(p, axis=0, keepdims=True)
                acc = acc * shift + dot(vT_ref[h, :, keys], p.astype(BF16))
                m = new_m
            oT_ref[h, :, q0 : q0 + tok] = acc / total
            lse_ref[h, :, q0 : q0 + tok] = m + jnp.log(total)
        return carry

    lax.fori_loop(0, heads, head, 0)


def pairs_of(i, tok, blocks, sub):
    out = []
    if i == 0:
        out.append((0, tok, 0, tok, False, True))
    edge = i == 0 or i == blocks - 1
    for j in range(i):
        out.append(((j + 1) * tok, tok, 0, tok, False, j == 0 or edge))
    for a in range(tok // sub):
        out.append(((i + 1) * tok + a * sub, sub, a * sub, tok - a * sub, True, edge))
    return out


def bwd_kernel(
    tok, blocks, heads, sub,
    k_ref, kT_ref, v_ref, q_ref, qT_ref, do_ref, doT_ref, oT_ref, lse_ref, dk_ref, dq_ref,
    dqT_out, dk_out, dv_out, delta,
):
    def head(h, carry):
        for i in range(blocks):
            sl = slice(i * tok, (i + 1) * tok)
            delta[:, sl] = jnp.sum(
                doT_ref[h, :, sl].astype(F32) * oT_ref[h, :, sl], axis=0, keepdims=True
            )
        dk_out[h] = jnp.zeros_like(dk_out[h])
        dv_out[h] = jnp.zeros_like(dv_out[h])
        dqT_out[h] = jnp.zeros_like(dqT_out[h])
        for i in range(blocks):
            q0 = i * tok
            for k0, kw, qo, qw, causal, docs in pairs_of(i, tok, blocks, sub):
                ks, qs = slice(k0, k0 + kw), slice(q0 + qo, q0 + qo + qw)
                s = dot(k_ref[h, ks, :], qT_ref[h, :, qs])
                p = jnp.exp(s - lse_ref[h, :, qs])
                docs_k = dk_ref[ks, :] if docs else None
                p = masked(p, docs_k, dq_ref[:, qs], k0 - tok, q0 + qo, causal, docs, 0.0)
                dp = dot(v_ref[h, ks, :], doT_ref[h, :, qs])
                ds = (p * (dp - delta[:, qs])).astype(BF16)
                dv_out[h, ks, :] += dot(p.astype(BF16), do_ref[h, qs, :])
                dk_out[h, ks, :] += dot(ds, q_ref[h, qs, :])
                dqT_out[h, :, qs] += dot(kT_ref[h, :, ks], ds)
        return carry

    lax.fori_loop(0, heads, head, 0)


def attend(k, qT, vT, docs_k, docs_q, tok):
    heads, hd, row = qT.shape
    return pl.pallas_call(
        functools.partial(fwd_kernel, tok, row // tok, heads),
        out_shape=[
            jax.ShapeDtypeStruct((heads, hd, row), F32),
            jax.ShapeDtypeStruct((heads, 1, row), F32),
        ],
        compiler_params=pltpu.CompilerParams(vmem_limit_bytes=VMEM_LIMIT),
    )(k, qT, vT, docs_k, docs_q)


def attend_back(k, kT, v, q, qT, do, doT, oT, lse, docs_k, docs_q, tok):
    heads, hd, row = qT.shape
    return pl.pallas_call(
        functools.partial(bwd_kernel, tok, row // tok, heads, tok // 2),
        out_shape=[
            jax.ShapeDtypeStruct((heads, hd, row), F32),
            jax.ShapeDtypeStruct(k.shape, F32),
            jax.ShapeDtypeStruct(k.shape, F32),
        ],
        scratch_shapes=[pltpu.VMEM((1, row), F32)],
        compiler_params=pltpu.CompilerParams(vmem_limit_bytes=VMEM_LIMIT),
    )(k, kT, v, q, qT, do, doT, oT, lse, docs_k, docs_q)


def per_device(residual, documents, gain_one, gain_two, w_qkv, w_out, w_up, w_down, cotangent):
    seq_count = lax.axis_size("seq")
    place = lax.axis_index("seq")
    narrow = residual[0]
    tok = narrow.shape[0]
    width = w_out.shape[0]
    row = seq_count * tok
    heads = H // seq_count
    mine = heads * HD
    scale = 1.0 / math.sqrt(HD)

    h_one = crms_norm(narrow, gain_one).astype(BF16)
    h_all = lax.all_gather(h_one, "seq", axis=0, tiled=True)
    row_docs = lax.all_gather(documents[0], "seq", axis=0, tiled=True)
    w_mine = lax.dynamic_slice_in_dim(w_qkv.reshape(width, 3, width), place * mine, mine, axis=2)
    packed = jnp.dot(h_all, w_mine.reshape(width, 3 * mine), preferred_element_type=F32)
    packed = packed.astype(BF16)
    tail = slice(row - tok, row)
    prior, prior_docs = passed_along((packed[tail, mine:], row_docs[tail]), "batch", 1)
    kv = jnp.concatenate([prior, packed[:, mine:]], axis=0)
    docs_k = jnp.concatenate([prior_docs, row_docs])[:, None]
    docs_q = row_docs[None]

    def by_head(flat):
        return flat.reshape(flat.shape[0], heads, HD).transpose(1, 0, 2)

    q = by_head(packed[:, :mine] * jnp.bfloat16(scale))
    k = by_head(kv[:, :mine])
    v = by_head(kv[:, mine:])
    qT, kT, vT = q.swapaxes(1, 2), k.swapaxes(1, 2), v.swapaxes(1, 2)
    oT, lse = attend(k, qT, vT, docs_k, docs_q, tok)
    o_rows = oT.astype(BF16).transpose(2, 0, 1).reshape(row, mine)
    attended = lax.all_to_all(o_rows, "seq", split_axis=0, concat_axis=1, tiled=True)

    branch_one = jnp.dot(attended, w_out, preferred_element_type=F32)
    middle = narrow + shrink(branch_one)
    h_two = crms_norm(middle, gain_two).astype(BF16)
    up_proj = jnp.dot(h_two, w_up, preferred_element_type=F32)
    gelu_out = jax.nn.gelu(up_proj).astype(BF16)
    branch_two = jnp.dot(gelu_out, w_down, preferred_element_type=F32)
    new_residual = middle + shrink(branch_two)
    grad_new = cotangent[0]
    grad_two = shrink_back(grad_new).astype(BF16)
    grad_w_down = jnp.einsum("tf,td->fd", gelu_out, grad_two, preferred_element_type=F32)
    grad_gelu = jnp.einsum("td,fd->tf", grad_two, w_down, preferred_element_type=F32)
    _, gelu_pull = jax.vjp(jax.nn.gelu, up_proj)
    grad_up = gelu_pull(grad_gelu)[0].astype(BF16)
    grad_w_up = jnp.einsum("td,tf->df", h_two, grad_up, preferred_element_type=F32)
    grad_h_two = jnp.einsum("tf,df->td", grad_up, w_up, preferred_element_type=F32)
    _, norm_pull_two = jax.vjp(crms_norm, middle, gain_two)
    grad_middle_norm, grad_gain_two = norm_pull_two(grad_h_two)
    grad_middle = grad_new + grad_middle_norm
    grad_one = shrink_back(grad_middle).astype(BF16)
    grad_w_out = jnp.einsum("td,te->de", attended, grad_one, preferred_element_type=F32)
    grad_attended = jnp.einsum("te,de->td", grad_one, w_out, preferred_element_type=F32)
    do_rows = lax.all_to_all(
        grad_attended.astype(BF16), "seq", split_axis=1, concat_axis=0, tiled=True
    )

    mlp_shares = [
        lax.psum_scatter(g.astype(BF16), "seq", scatter_dimension=0, tiled=True)
        for g in (grad_w_down, grad_w_up, grad_w_out)
    ]
    mlp_totals = lax.psum(tuple(mlp_shares), "batch")

    do = by_head(do_rows)
    doT = do.swapaxes(1, 2)
    dqT, dk, dv = attend_back(k, kT, v, q, qT, do, doT, oT, lse, docs_k, docs_q, tok)
    back_k, back_v = passed_along((dk[:, :tok].astype(BF16), dv[:, :tok].astype(BF16)), "batch", -1)

    def with_tail(own, back):
        return jnp.concatenate([own[:, tok:-tok], own[:, -tok:] + back.astype(F32)], axis=1)

    def rows_of(heads_first):
        return heads_first.transpose(1, 0, 2).reshape(row, mine).astype(BF16)

    grad_packed = jnp.concatenate(
        [
            rows_of(dqT.swapaxes(1, 2) * scale),
            rows_of(with_tail(dk, back_k)),
            rows_of(with_tail(dv, back_v)),
        ],
        axis=1,
    )
    grad_w_mine = jnp.einsum("td,tf->df", h_all, grad_packed, preferred_element_type=F32)
    grad_h_part = jnp.einsum(
        "tf,df->td", grad_packed, w_mine.reshape(width, 3 * mine), preferred_element_type=F32
    )
    grad_h_one = lax.psum_scatter(
        grad_h_part.astype(BF16), "seq", scatter_dimension=0, tiled=True
    ).astype(F32)
    _, norm_pull_one = jax.vjp(crms_norm, narrow, gain_one)
    grad_narrow_norm, grad_gain_one = norm_pull_one(grad_h_one)
    residual_grad = grad_middle + grad_narrow_norm
    grad_w_rows = lax.all_to_all(
        grad_w_mine.astype(BF16), "seq", split_axis=0, concat_axis=1, tiled=True
    )
    grad_w_rows = lax.psum(grad_w_rows, "batch").astype(F32)
    share = width // seq_count
    grad_w_qkv = (
        grad_w_rows.reshape(share, seq_count, 3, mine)
        .transpose(0, 2, 1, 3)
        .reshape(share, 3 * width)
    )
    gains = jnp.stack([grad_gain_one, grad_gain_two])
    gains = lax.psum(
        lax.psum_scatter(gains, "seq", scatter_dimension=1, tiled=True), "batch"
    )
    return (
        new_residual[None],
        residual_grad[None],
        gains[0],
        gains[1],
        grad_w_qkv,
        mlp_totals[2].astype(F32),
        mlp_totals[1].astype(F32),
        mlp_totals[0].astype(F32),
    )


def solution(mesh):
    placed = (
        P("batch", "seq", None),
        P("batch", "seq"),
        P(),
        P(),
        P(),
        P(),
        P(),
        P(),
        P("batch", "seq", None),
    )
    return jax.shard_map(
        per_device,
        mesh=mesh,
        in_specs=placed,
        out_specs=(
            P("batch", "seq", None),
            P("batch", "seq", None),
            P("seq"),
            P("seq"),
            P("seq", None),
            P("seq", None),
            P("seq", None),
            P("seq", None),
        ),
        check_vma=False,
    )
```

time: 1090 us -> 593 us (0.54)
  matrix products: 457 us -> 63 us
  local copies, waits for them, and re-layouts: 170 us -> 68.8 us
  other arithmetic: 106 us -> 36.1 us
  Pallas kernels: 0 us -> 49.6 us
  waiting for transfers between devices: 270 us -> 303 us
  blocking collectives: 49.8 us -> 28 us
    dot_general x57 -> x12, matrix products: 457 us -> 63 us  [the longest x1 9.38 us: per_device(): jnp.einsum('td,fd->tf', grad_two, w_down, preferred_element_type=F32)]
    reduce_scatter x4, waiting for transfers between devices: 63.3 us -> 130 us  [the longest x3 118 us: per_device(): lax.psum_scatter(g.astype(BF16), 'seq', scatter_dimension=0, tiled=True)]
    psum x1, waiting for transfers between devices: 177 us -> 122 us  [per_device(): grad_w_rows = lax.psum(grad_w_rows, 'batch').astype(F32)]
    pallas_call x0 -> x2, Pallas kernels: none -> 49.6 us  [the longest x1 31.4 us: attend_back(): pl.pallas_call(functools.partial(bwd_kernel, tok, row // tok, heads, tok...]
    concatenate x8 -> x0, local copies, waits for them, and re-layouts: 34.8 us -> none  [the longest x2 8.73 us: per_device(): jnp.concatenate([prior_keys[None], near_keys.reshape(seq_count, tok_rows,...]
    reduce_sum x6 -> x1, other arithmetic: 36.4 us -> 1.79 us  [crms_norm(): gain_vec * full_vec]
    concatenate x8 -> x2, other arithmetic: 23.1 us -> 1.42 us  [the longest x1 1.42 us: per_device(): kv = jnp.concatenate([prior, packed[:, mine:]], axis=0)]
    all_gather x5 -> x0, local copies, waits for them, and re-layouts: 19.5 us -> none  [the longest x1 4.81 us: per_device(): lax.all_gather(value_rows, 'seq', axis=0, tiled=True)]
  transfers between devices with their start and end apart: 17 -> 14, of which waited for: 4 -> 13; matrix products, arithmetic and copies ran while one was open for 65% -> 14% of each run, Pallas kernels for 0% -> 0%
where the time goes in v1:
time: 593 us; the launch traced here: 584 us
  waiting for transfers between devices  303 us (51%)
  local copies, waits for them, and re-layouts  68.8 us (12%)
  matrix products  63 us (11%)
  Pallas kernels  49.6 us (8%)
  other arithmetic  36.1 us (6%)
  blocking collectives  28 us (5%)
  starting transfers between devices  19.9 us (3%)
  between operations  15 us (3%)
    psum x1, waiting for transfers between devices, per_device(): grad_w_rows = lax.psum(grad_w_rows, 'batch').astype(F32)  122 us
    reduce_scatter x3, waiting for transfers between devices, per_device(): lax.psum_scatter(g.astype(BF16), 'seq', scatter_dimension=0, tiled=True)  118 us
    pallas_call x1, Pallas kernels, attend_back(): pl.pallas_call(functools.partial(bwd_kernel, tok, row // tok, heads, tok...  31.4 us
    unnamed x59, local copies, waits for them, and re-layouts  28.9 us
    psum x1, blocking collectives, per_device(): lax.psum(lax.psum_scatter(gains, 'seq', scatter_dimension=1, tiled=True),...  21.9 us
    pallas_call x1, Pallas kernels, attend(): pl.pallas_call(functools.partial(fwd_kernel, tok, row // tok, heads), out...  18.3 us
    ppermute x4, waiting for transfers between devices, passed_along(): return lax.ppermute(block, axis, route)  18.2 us
    all_gather x1, waiting for transfers between devices, per_device(): h_all = lax.all_gather(h_one, 'seq', axis=0, tiled=True)  13.2 us
  transfers between devices with their start and end apart: 14, of which 13 were waited for; matrix products, arithmetic and copies ran while one was open for 14% of the time, Pallas kernels for 0%

profile of v1, /device:TPU:0, one launch (start us, length us, event | category | flops | bytes accessed | tf_op | source)
XLA Modules:
  0.0 583.6 jit_solution(2422482493534964782)
XLA Ops:
  7.2 3.6 copy.92
  14.7 6.1 %all-gather.dq_ref = s32[1,2048]{1,0:T(1,128)S(1)} all-gather(s32[1,512]{1,0:T(1,128)S(1)} %copy-done.21), channel_id=2, replica_groups=mesh['seq'=4,'batch'=8] {'seq'}, dimensions={1}, use_global_device_ids=true | all-gather | bytes 10240 | tf_op jit(solution)/shard_map/all_gather | solution.py:178
  22.9 5.9 %copy.94 = bf16[768,2304]{0,1:T(8,128)(2,1)} copy(bf16[768,2304]{1,0:T(8,128)(2,1)} %param.13) | data formatting | bytes 7077888 | tf_op args[4]
  32.9 13.2 %all-gather.3.cloned.1.call-done = bf16[2048,768]{1,0:T(8,128)(2,1)} async-done(((bf16[512,768]{1,0:T(8,128)(2,1)}), bf16[2048,768]{1,0:T(8,128)(2,1)}) %all-gather.3.cloned.1.call-update) | async-done | bytes 3145744 | tf_op jit(solution)/shard_map/all_gather | solution.py:177
  46.1 4.1 convolution_convert_fusion.3
  52.9 11.5 %collective-permute-done = bf16[512,384]{0,1:T(8,128)(2,1)S(1)} collective-permute-done((bf16[512,384]{0,1:T(8,128)(2,1)S(1)}, bf16[512,384]{0,1:T(8,128)(2,1)S(1)}, u32[]{:S(2)}, u32[]{:S(2)}) %collective-permute-start) | collective-permute-done | bytes 393248 | tf_op jit(solution)/shard_map/ppermute | solution.py:22
  68.5 18.3 %shard_map.152 = (f32[3,64,2048]{2,1,0:T(8,128)}, f32[3,1,2048]{2,1,0:T(1,128)}) custom-call(bf16[3,2560,64]{2,1,0:T(8,128)(2,1)} %copy.95.k_ref, bf16[3,64,2048]{2,1,0:T(8,128)(2,1)} %bitcast.79, bf16[3,64,2560]{2,1,0:T(8,128)(2,1)} %bitcast.82, s32[2560,1]{1,0:T(8,128)} %broadcast_in_dim.48.dk_ref, s32[1,2048]{1,0:T(1,128)} %copy-done.18), custom_call_target="tpu_custom_call" | custom-call | tf_op jit(solution)/shard_map/pallas_call | solution.py:141
  94.3 4.7 all-to-all-start
  101.3 4.9 copy.99
  106.2 4.5 all-to-all-done
  116.3 4.7 fusion.26
  121.1 9.4 %fusion.6 = bf16[512,3072]{1,0:T(8,128)(2,1)S(1)} fusion(f32[512,3072]{1,0:T(8,128)S(1)} %fusion.26, bf16[3072,768]{1,0:T(8,128)(2,1)} %param.16, f32[512,767]{1,0:T(8,128)S(1)} %bitcast.90, f32[512]{0:T(512)S(1)} %broadcast_multiply_fusion.1), kind=kOutput, calls=%fused_computation.8 | convolution fusion | flops 2448162816 | bytes 15728640 | tf_op jit(solution)/shard_map/td,fd->tf/dot_general | solution.py:209
  139.7 4.2 all-to-all-start.1
  148.4 7.2 %all-to-all-done.1 = bf16[512,4,192]{0,2,1:T(8,128)(2,1)} async-done(((bf16[512,4,192]{0,2,1:T(8,128)(2,1)}), bf16[512,4,192]{0,2,1:T(8,128)(2,1)}, u32[]{:S(2)}, u32[]{:S(2)}) %all-to-all-start.1) | async-done | bytes 786464 | tf_op jit(solution)/shard_map/all_to_all | solution.py:220
  161.9 31.4 %shard_map.153 = (f32[3,64,2048]{2,1,0:T(8,128)}, f32[3,2560,64]{2,1,0:T(8,128)}, f32[3,2560,64]{2,1,0:T(8,128)}) custom-call(bf16[3,2560,64]{2,1,0:T(8,128)(2,1)} %copy.95.k_ref, bf16[3,64,2560]{2,1,0:T(8,128)(2,1)} %bitcast.85, bf16[3,2560,64]{2,1,0:T(8,128)(2,1)} %bitcast.86, bf16[3,2048,64]{2,1,0:T(8,128)(2,1)} %copy.104.q_ref, ...), custom_call_target="tpu_custom_call" | custom-call | tf_op jit(solution)/shard_map/pallas_call | solution.py:153
  203.1 4.8 collective-permute-done.2
  220.4 5.9 %convolution_convert_fusion.2 = bf16[2048,768]{1,0:T(8,128)(2,1)} fusion(bf16[768,576]{0,1:T(8,128)(2,1)S(1)} %bitcast.97, bf16[2048,192]{0,1:T(8,128)(2,1)} %bitcast.102, bf16[2048,192]{0,1:T(8,128)(2,1)} %bitcast.100, bf16[2048,192]{0,1:T(8,128)(2,1)} %bitcast.98), kind=kOutput, calls=%fused_computation.12 | convolution fusion | flops 1820590080 | bytes 6389760 | tf_op jit(solution)/shard_map/tf,df->td/dot_general | solution.py:250
  226.4 3.6 convolution_convert_fusion.4
  230.0 9.3 %convolution_convert_fusion = bf16[3072,768]{1,0:T(8,128)(2,1)} fusion(f32[512,767]{1,0:T(8,128)} %bitcast.89, f32[512]{0:T(512)S(1)} %broadcast_multiply_fusion.1, f32[512,3072]{1,0:T(8,128)} %copy-done.22), kind=kOutput, calls=%fused_computation.10 | convolution fusion | flops 2433220608 | bytes 12582912 | tf_op jit(solution)/shard_map/tf,td->fd/dot_general | solution.py:208
  239.6 7.3 %convolution_convert_fusion.1 = bf16[768,3072]{1,0:T(8,128)(2,1)} fusion(bf16[512,3072]{1,0:T(8,128)(2,1)} %copy-done.23, f32[512]{0:T(512)S(1)} %fusion.22, f32[768]{0:T(1024)S(1)} %copy-done.20, f32[512,1]{1,0:T(8,128)S(1)} %copy.98, f32[512,767]{1,0:T(8,128)} %get-tuple-element.69), kind=kOutput, calls=%fused_computation.11 | convolution fusion | flops 2419851264 | bytes 9442304 | tf_op jit(solution)/shard_map/td,tf->df/dot_general | solution.py:212
  247.0 4.6 convolution_convert_fusion.5
  252.9 3.5 all-to-all-start.2
  256.5 11.7 %reduce-scatter.8.cloned.1.call-done = bf16[512,768]{1,0:T(8,128)(2,1)} async-done(((bf16[2048,768]{1,0:T(8,128)(2,1)}), bf16[512,768]{1,0:T(8,128)(2,1)}) %reduce-scatter.8.cloned.1.call-update) | async-done | bytes 786448 | tf_op jit(solution)/shard_map/reduce_scatter | solution.py:253
  278.3 3.2 reshape.152
  281.5 17.4 %reduce-scatter.10.cloned.1.call-done = bf16[192,768]{1,0:T(8,128)(2,1)} async-done(((bf16[768,768]{1,0:T(8,128)(2,1)}), bf16[192,768]{1,0:T(8,128)(2,1)}) %reduce-scatter.10.cloned.1.call-update) | async-done | bytes 294928 | tf_op jit(solution)/shard_map/reduce_scatter | solution.py:225
  298.9 50.2 %reduce-scatter.14.cloned.1.call-done = bf16[768,768]{1,0:T(8,128)(2,1)} async-done(((bf16[3072,768]{1,0:T(8,128)(2,1)}), bf16[768,768]{1,0:T(8,128)(2,1)}) %reduce-scatter.14.cloned.1.call-update) | async-done | bytes 1179664 | tf_op jit(solution)/shard_map/reduce_scatter | solution.py:225
  349.1 50.4 %reduce-scatter.12.cloned.1.call-done = bf16[192,3072]{1,0:T(8,128)(2,1)} async-done(((bf16[768,3072]{1,0:T(8,128)(2,1)}), bf16[192,3072]{1,0:T(8,128)(2,1)}) %reduce-scatter.12.cloned.1.call-update) | async-done | bytes 1179664 | tf_op jit(solution)/shard_map/reduce_scatter | solution.py:225
  399.6 7.5 %fusion.34 = (f32[512]{0:T(512)S(1)}, f32[512,768]{1,0:T(8,128)S(1)}) fusion(bf16[3072,768]{1,0:T(8,128)(2,1)} %param.16, f32[512,3072]{1,0:T(8,128)} %copy-done.22), kind=kOutput, calls=%fused_computation.83 | convolution fusion | flops 2430467584 | bytes 12584960 | tf_op jit(solution)/shard_map/dot_general | solution.py:204
  408.5 4.9 copy.112
  417.7 5.6 reduce-scatter.16.cloned.1.call-done
  424.3 21.9 %psum.35 = f32[2,192]{1,0:T(2,128)S(1)} all-reduce(f32[2,192]{1,0:T(2,128)S(1)} %copy.115), channel_id=1, replica_groups=mesh['seq'=4,'batch'=8] {'batch'}, use_global_device_ids=true, to_apply=%region_14.0 | all-reduce | flops 384 | bytes 3072 | tf_op jit(solution)/shard_map/psum | solution.py:270
  446.8 121.7 %all-reduce.5.cloned.1.call-done = (bf16[192,2304]{1,0:T(8,128)(2,1)}, bf16[192,768]{1,0:T(8,128)(2,1)}, bf16[192,3072]{1,0:T(8,128)(2,1)}, bf16[768,768]{1,0:T(8,128)(2,1)}) async-done(((bf16[192,2304]{1,0:T(8,128)(2,1)}, bf16[192,768]{1,0:T(8,128)(2,1)}, bf16[192,3072]{1,0:T(8,128)(2,1)}, bf16[768,768]{1,0:T(8,128)(2,1)}), (bf16[192,2304]{1,0:T(8,128)(2,1)}, bf16[192,768]{1,0:T(8,128)(2,1)}, ...) | async-done | bytes 3538960 | tf_op jit(solution)/shard_map/psum | solution.py:262
  (150 shorter events, 101.3 us)
Async XLA Ops:
  7.2 103.5 %copy-start = (bf16[768,768]{1,0:T(8,128)(2,1)S(1)}, bf16[768,768]{1,0:T(8,128)(2,1)}, u32[]{:S(2)}) copy-start(bf16[768,768]{1,0:T(8,128)(2,1)} %param.14) | copy-start | bytes 3538948
  7.2 38.9 %all-gather.3.cloned.1.call-start = ((), (), s32[]{:S(2)}) async-start(), calls=%async_computation.8 | async-start | bytes 3932160 | tf_op jit(solution)/shard_map/all_gather | solution.py:177
  10.8 2.7 copy-start.19
  20.8 10.0 %copy-start.18 = (s32[1,2048]{1,0:T(1,128)}, s32[1,2048]{1,0:T(1,128)S(1)}, u32[]{:S(2)}) copy-start(s32[1,2048]{1,0:T(1,128)S(1)} %all-gather.dq_ref) | copy-start | bytes 24580
  20.8 10.0 %collective-permute-start.1 = (s32[512]{0:T(512)S(1)}, s32[512]{0:T(512)S(1)}, u32[]{:S(2)}, u32[]{:S(2)}) collective-permute-start(s32[512]{0:T(512)S(1)} %bitcast.108), channel_id=1, source_target_pairs={{7,0},{0,1},{1,2},{2,3},{3,4},{4,5},{5,6},{6,7},{15,8},{8,9},{9,10... | collective-permute-start | bytes 6152 | tf_op jit(solution)/shard_map/ppermute | solution.py:22
  50.4 14.0 %collective-permute-start = (bf16[512,384]{0,1:T(8,128)(2,1)S(1)}, bf16[512,384]{0,1:T(8,128)(2,1)S(1)}, u32[]{:S(2)}, u32[]{:S(2)}) collective-permute-start(bf16[512,384]{0,1:T(8,128)(2,1)S(1)} %slice.69), channel_id=1, source_target_pairs={{7,0},{0,1},{1,2},{2,3},{3,4},{4,5},{5,6},{6,7},{15,8},{8,9},{9,10... | collective-permute-start | bytes 1179656 | tf_op jit(solution)/shard_map/ppermute | solution.py:22
  94.3 16.4 %all-to-all-start = ((bf16[4,512,192]{1,2,0:T(8,128)(2,1)}), bf16[4,512,192]{1,2,0:T(8,128)(2,1)}, u32[]{:S(2)}, u32[]{:S(2)}) async-start(bf16[4,512,192]{1,2,0:T(8,128)(2,1)} %copy.97), calls=%async_computation | async-start | bytes 1572864 | tf_op jit(solution)/shard_map/all_to_all | solution.py:197
  116.3 4.8 copy-start.10
  116.3 14.2 %slice-start.2 = ((s8[4718592]{0:T(1024)(128)(4,1)}), s8[4194304]{0:T(1024)(128)(4,1)S(1)}, s32[]{:S(2)}) async-start(s8[4718592]{0:T(1024)(128)(4,1)} %bitcast.111), calls=%async_computation.17 | async-start | bytes 8388608
  121.0 9.4 %copy-start.22 = (f32[512,3072]{1,0:T(8,128)}, f32[512,3072]{1,0:T(8,128)S(1)}, u32[]{:S(2)}) copy-start(f32[512,3072]{1,0:T(8,128)S(1)} %fusion.26) | copy-start | bytes 18874372
  121.1 9.4 %slice-start.3 = ((s8[4718592]{0:T(1024)(128)(4,1)}), s8[524288]{0:T(1024)(128)(4,1)S(1)}, s32[]{:S(2)}) async-start(s8[4718592]{0:T(1024)(128)(4,1)} %bitcast.111), calls=%async_computation.18 | async-start | bytes 1048576
  130.5 2.8 copy-start.23
  137.3 6.8 %copy-start.4 = (bf16[2048,192]{0,1:T(8,128)(2,1)S(1)}, bf16[2048,192]{0,1:T(8,128)(2,1)}, u32[]{:S(2)}) copy-start(bf16[2048,192]{0,1:T(8,128)(2,1)} %slice_multiply_fusion) | copy-start | bytes 2359300
  139.7 15.9 %all-to-all-start.1 = ((bf16[512,4,192]{0,2,1:T(8,128)(2,1)}), bf16[512,4,192]{0,2,1:T(8,128)(2,1)}, u32[]{:S(2)}, u32[]{:S(2)}) async-start(bf16[512,4,192]{0,2,1:T(8,128)(2,1)} %bitcast.94), calls=%async_computation.1 | async-start | bytes 1572864 | tf_op jit(solution)/shard_map/all_to_all | solution.py:220
  143.9 124.3 %reduce-scatter.8.cloned.1.call-start = ((), (), s32[]{:S(2)}) async-start(), calls=%async_computation.9 | async-start | bytes 3932160 | tf_op jit(solution)/shard_map/reduce_scatter | solution.py:253
  193.3 4.1 copy-start.14
  195.8 2.7 copy-start.6
  195.8 12.1 %collective-permute-start.2 = (bf16[3,512,64]{2,1,0:T(8,128)(2,1)S(1)}, bf16[3,512,64]{2,1,0:T(8,128)(2,1)S(1)}, u32[]{:S(2)}, u32[]{:S(2)}) collective-permute-start(bf16[3,512,64]{2,1,0:T(8,128)(2,1)S(1)} %slice.78), channel_id=1, source_target_pairs={{1,0},{2,1},{3,2},{4,3},{5,4},{6,5},{7,6},{0,7},{9,8},{10,9},{11,1... | collective-permute-start | bytes 589832 | tf_op jit(solution)/shard_map/ppermute | solution.py:22
  197.4 2.4 copy-start.11
  200.9 8.2 %slice-start = ((bf16[3,2560,64]{2,1,0:T(8,128)(2,1)}), bf16[3,1536,64]{2,1,0:T(8,128)(2,1)S(1)}, s32[]{:S(2)}) async-start(bf16[3,2560,64]{2,1,0:T(8,128)(2,1)} %copy-done.6), calls=%async_computation.15 | async-start | bytes 2359296 | tf_op jit(solution)/shard_map/slice | solution.py:236
  201.5 13.6 %collective-permute-start.3 = (bf16[3,512,64]{2,1,0:T(8,128)(2,1)}, bf16[3,512,64]{2,1,0:T(8,128)(2,1)}, u32[]{:S(2)}, u32[]{:S(2)}) collective-permute-start(bf16[3,512,64]{2,1,0:T(8,128)(2,1)} %slice.80), channel_id=1, source_target_pairs={{1,0},{2,1},{3,2},{4,3},{5,4},{6,5},{7,6},{0,7},{9,8},{10,9},{11,1... | collective-permute-start | bytes 589832 | tf_op jit(solution)/shard_map/ppermute | solution.py:22
  210.6 5.8 slice-start.1
  217.9 2.5 copy-start.17
  226.3 72.6 %reduce-scatter.10.cloned.1.call-start = ((), (), s32[]{:S(2)}) async-start(), calls=%async_computation.10 | async-start | bytes 1474560 | tf_op jit(solution)/shard_map/reduce_scatter | solution.py:225
  230.0 119.2 %reduce-scatter.14.cloned.1.call-start = ((), (), s32[]{:S(2)}) async-start(), calls=%async_computation.12 | async-start | bytes 5898240 | tf_op jit(solution)/shard_map/reduce_scatter | solution.py:225
  239.3 160.2 %reduce-scatter.12.cloned.1.call-start = ((), (), s32[]{:S(2)}) async-start(), calls=%async_computation.11 | async-start | bytes 5898240 | tf_op jit(solution)/shard_map/reduce_scatter | solution.py:225
  252.9 20.9 %all-to-all-start.2 = ((bf16[4,192,576]{2,1,0:T(8,128)(2,1)}), bf16[4,192,576]{2,1,0:T(8,128)(2,1)S(1)}, u32[]{:S(2)}, u32[]{:S(2)}) async-start(bf16[4,192,576]{2,1,0:T(8,128)(2,1)} %bitcast.36), calls=%async_computation.3 | async-start | bytes 1966080 | tf_op jit(solution)/shard_map/all_to_all | solution.py:259
  256.4 167.0 %reduce-scatter.16.cloned.1.call-start = ((), (), s32[]{:S(2)}) async-start(), calls=%async_computation.13 | async-start | bytes 491520
  271.0 297.6 %all-reduce.5.cloned.1.call-start = ((), (), s32[]{:S(2)}) async-start(), calls=%async_computation.14 | async-start | bytes 7077888 | tf_op jit(solution)/shard_map/psum | solution.py:262
  399.6 7.5 %copy-start.3 = (f32[512,767]{1,0:T(8,128)S(1)}, f32[512,767]{1,0:T(8,128)}, u32[]{:S(2)}) copy-start(f32[512,767]{1,0:T(8,128)} %get-tuple-element.69) | copy-start | bytes 4712452
  408.4 4.9 copy-start.13
  568.5 4.4 copy-start.16
  (10 other events, 14.8 us)
Sparse Core Ops, SparseCore 0:
  14.8 31.2 all-gather.2
  226.5 41.6 reduce-scatter.7
  271.5 27.3 reduce-scatter.9
  301.3 47.8 reduce-scatter.13
  351.7 47.8 reduce-scatter.11
  402.5 20.8 reduce-scatter.15
  427.9 140.5 all-reduce.4
